TPU v7x, 128 devices: a whole 4x4x4 slice. The times are simulated.
128 devices in a mesh: mp: 8 (over z, x_lo), dp: 16 (over x_hi, y, core).
Axes of the slice: x: 4 (x_hi: 2, x_lo: 2; x = x_hi * 2 + x_lo), y: 4, z: 4, core: 2. Of those that a mesh axis runs over, the one named last changes fastest.
Arguments:
- volume: bfloat16 [16, 64, 64, 2048], P('dp', 'mp'), may hold values from -6 to 6
- kernel_a: bfloat16 [3, 3, 3, 32, 64], replicated, may hold values from -0.21875 to 0.21875
- kernel_b: bfloat16 [3, 3, 3, 64, 128], P(None, None, None, 'mp'), may hold values from -0.15625 to 0.15625
- cotangent: bfloat16 [16, 16, 16, 16, 128], P('dp', None, None, None, 'mp'), may hold values from -6 to 6
Outputs:
- features: bfloat16 [16, 16, 16, 16, 128], P('dp', None, None, None, 'mp')
- grad_a: float32 [3, 3, 3, 32, 64], replicated
- grad_b: float32 [3, 3, 3, 64, 128], P(None, None, None, 'mp')
All inputs are finite; a program needn't handle non-finite values.
Results may differ from a plain program's by a relative error of at most 0.0049.
Values may be sent and summed in bfloat16 or wider, within the bound.
A program may use at most 192 MiB of HBM per device.

v0:
```python
import math
import jax
import jax.numpy as jnp
from jax import lax
from jax.sharding import PartitionSpec as P

GRID = 64


def shifted(array, axis, by):
    size = lax.axis_size(axis)
    pairs = [(i, i + by) for i in range(size) if 0 <= i + by < size]
    return lax.ppermute(array, axis, pairs)


def forward_conv(padded, kernel):
    return lax.conv_general_dilated(
        padded,
        kernel,
        (2, 2, 2),
        "VALID",
        dimension_numbers=("NDHWC", "DHWIO", "NDHWC"),
        preferred_element_type=jnp.float32,
    )


def kernel_grad(padded, grads):
    result = lax.conv_general_dilated(
        padded,
        grads,
        (1, 1, 1),
        "VALID",
        rhs_dilation=(2, 2, 2),
        dimension_numbers=("CDHWN", "IDHWO", "NDHWC"),
        preferred_element_type=jnp.float32,
    )
    return jnp.transpose(result, (1, 2, 3, 0, 4))


def input_grad(grads, kernel, first_low):
    flipped = kernel[::-1, ::-1, ::-1]
    return lax.conv_general_dilated(
        grads,
        flipped,
        (1, 1, 1),
        ((first_low, 2), (1, 2), (1, 2)),
        lhs_dilation=(2, 2, 2),
        dimension_numbers=("NDHWC", "DHWOI", "NDHWC"),
        preferred_element_type=jnp.float32,
    )


def pad_sides(field):
    return jnp.pad(field, ((0, 0), (0, 0), (1, 0), (1, 0), (0, 0)))


def pad_low(field):
    return jnp.pad(field, ((0, 0), (1, 0), (1, 0), (1, 0), (0, 0)))


def shards(volume, kernel_a, kernel_b, cotangent):
    samp_local = volume.shape[0]
    planes = volume.shape[1]
    edge = volume.shape[2]
    in_chan = kernel_a.shape[3]
    field = volume.reshape(samp_local, planes, edge, edge, in_chan)
    below = shifted(field[:, planes - 1 :], "mp", 1)
    padded_x = pad_sides(jnp.concatenate([below, field], axis=1))
    pre = forward_conv(padded_x, kernel_a)
    hidden = jnp.where(pre > 0, pre, 0.3 * pre).astype(jnp.bfloat16)
    grouped = lax.all_to_all(hidden, "mp", split_axis=4, concat_axis=1, tiled=True)
    padded_h = pad_low(grouped)
    partial_out = forward_conv(padded_h, kernel_b)
    features = lax.psum_scatter(partial_out, "mp", scatter_dimension=4, tiled=True).astype(
        jnp.bfloat16
    )
    upstream = lax.all_gather(cotangent, "mp", axis=4, tiled=True)
    local_b = kernel_grad(padded_h, upstream)
    back_group = input_grad(upstream, kernel_b, 1).astype(jnp.bfloat16)
    back = lax.all_to_all(back_group, "mp", split_axis=1, concat_axis=4, tiled=True)
    delta = (back.astype(jnp.float32) * jnp.where(pre > 0, 1.0, 0.3)).astype(jnp.bfloat16)
    local_a = kernel_grad(padded_x, delta)
    total_a = lax.psum(local_a, ("mp", "dp"))
    total_b = lax.psum(local_b, "dp")
    samples_all = samp_local * lax.axis_size("dp")
    grad_a = total_a / math.sqrt(samples_all * (GRID // 2) ** 3)
    grad_b = total_b / math.sqrt(samples_all * (GRID // 4) ** 3)
    return (features, grad_a, grad_b)


def solution(mesh):
    return jax.shard_map(
        shards,
        mesh=mesh,
        in_specs=(
            P("dp", "mp", None, None),
            P(),
            P(None, None, None, "mp", None),
            P("dp", None, None, None, "mp"),
        ),
        out_specs=(P("dp", None, None, None, "mp"), P(), P(None, None, None, "mp", None)),
        check_vma=False,
    )
```

profile of v0, /device:TPU:1, one launch (start us, length us, event | category | flops | bytes accessed | tf_op | source)
XLA Modules:
  0.0 838.3 jit_solution(7763710412680146833)
XLA Ops:
  7.2 4.9 copy.124
  14.2 4.0 collective-permute-start
  18.2 31.5 %copy.127 = bf16[1,8,64,64,32]{4,0,3,2,1:T(2,128)(2,1)} copy(bf16[1,8,64,64,32]{2,4,3,1,0:T(8,128)(2,1)} %bitcast.69) | data formatting | bytes 4194304 | tf_op jit(solution)/shard_map/reshape | solution.py:66
  52.4 58.2 %pad_maximum_fusion = bf16[1,9,64,64,32]{4,0,3,2,1:T(2,128)(2,1)} fusion(bf16[1,8,64,64,32]{4,0,3,2,1:T(2,128)(2,1)} %copy.127, bf16[1,1,64,64,32]{4,0,3,2,1:T(2,128)(2,1)S(1)} %copy.126), kind=kLoop, calls=%fused_computation.4 | loop fusion | flops 1179648 | bytes 4718592 | tf_op jit(solution)/shard_map/concatenate | solution.py:68
  110.6 33.5 %copy.128 = bf16[1,9,64,64,32]{3,4,2,1,0:T(8,128)(2,1)} copy(bf16[1,9,64,64,32]{4,0,3,2,1:T(2,128)(2,1)} %pad_maximum_fusion) | data formatting | bytes 4718592 | tf_op jit(solution)/shard_map/concatenate | solution.py:68
  144.1 9.2 %copy.159 = bf16[9,64,1,64,32]{1,4,3,0,2:T(8,128)(2,1)} copy(bf16[9,64,1,64,32]{3,4,2,1,0:T(8,128)(2,1)} %bitcast.72) | data formatting | bytes 4718592
  153.3 6.1 pad.4.clone
  159.4 15.6 %copy.131 = bf16[9,64,1,8,10,32]{5,3,4,1,0,2:T(8,128)(2,1)} copy(bf16[9,64,1,8,10,32]{1,5,4,3,0,2:T(8,128)(2,1)} %bitcast.67) | data formatting | bytes 5898240 | tf_op jit(solution)/shard_map/conv_general_dilated | solution.py:17
  177.4 12.0 %compare_select_fusion = (f32[4,32,8,5,64]{4,2,3,1,0:T(8,128)}, bf16[4,32,8,5,64]{4,2,3,1,0:T(8,128)(2,1)S(1)}) fusion(pred[8,5]{0,1:T(8,128)(4,1)S(1)} %copy-done.6, bf16[3,3,3,32,64]{4,3,2,1,0:T(8,128)(2,1)S(1)} %copy-done, bf16[9,64,1,7,2,32]{5,3,4,1,0,2:T(8,128)(2,1)S(1)} %slice.12, bf16[9,64,1,8,10,32]{5,3,4,1,0,2:T(8,128)(2,1)} %copy.131), kind=kOutput, calls=%fused_computation.20 | convolution fusion | flops 572915712 | bytes 5541928 | tf_op jit(solution)/shard_map/conv_general_dilated | solution.py:17
  195.8 6.1 all-to-all-start
  202.0 3.9 copy.140
  216.9 3.4 copy.160
  220.4 4.0 pad.6.clone
  224.4 12.8 %copy.138 = bf16[32,32,1,8,6,8]{5,3,4,1,0,2:T(8,128)(2,1)} copy(bf16[32,32,1,8,6,8]{1,5,4,3,0,2:T(8,128)(2,1)} %bitcast.73) | data formatting | bytes 1572864 | tf_op jit(solution)/shard_map/conv_general_dilated | solution.py:17
  240.6 12.3 %broadcast_select_fusion = f32[16,16,8,3,128]{4,2,3,1,0:T(8,128)S(1)} fusion(pred[8,3]{0,1:T(4,128)(4,1)S(1)} %copy-done.7, bf16[3,3,3,8,128]{4,3,2,1,0:T(8,128)(2,1)S(1)} %copy-done.5, bf16[32,32,1,7,2,8]{5,3,4,1,0,2:T(8,128)(2,1)S(1)} %slice.14, bf16[32,32,1,8,6,8]{5,3,4,1,0,2:T(8,128)(2,1)} %copy.138), kind=kOutput, calls=%fused_computation.30 | convolution fusion | flops 329662464 | bytes 4216856 | tf_op jit(solution)/shard_map/conv_general_dilated | solution.py:17
  255.2 23.8 %copy.153 = bf16[1,32,32,32,8]{4,0,3,2,1:T(2,128)(2,1)} copy(bf16[1,32,32,32,8]{3,4,2,1,0:T(8,128)(2,1)S(1)} %bitcast.71) | data formatting | bytes 1048576 | tf_op jit(solution)/shard_map/all_to_all | solution.py:71
  279.0 97.7 %all-gather.2.cloned.1.call-done = bf16[1,16,16,16,128]{3,2,1,0,4:T(8,128)(2,1)} async-done(((bf16[1,16,16,16,16]{3,2,1,0,4:T(8,128)(2,1)}), bf16[1,16,16,16,128]{3,2,1,0,4:T(8,128)(2,1)}) %all-gather.2.cloned.1.call-update) | async-done | bytes 1048592 | tf_op jit(solution)/shard_map/all_gather | solution.py:77
  376.7 10.0 %copy.141 = bf16[1,16,16,16,128]{4,3,2,1,0:T(8,128)(2,1)S(1)} copy(bf16[1,16,16,16,128]{3,2,1,0,4:T(8,128)(2,1)} %all-gather.2.cloned.1.call-done) | data formatting | bytes 2097152 | tf_op jit(solution)/shard_map/all_gather | solution.py:77
  387.9 14.3 %fusion.17 = bf16[32,32,8,6,8]{4,2,3,1,0:T(8,128)(2,1)} fusion(bf16[3,3,3,8,128]{4,3,2,1,0:T(8,128)(2,1)S(1)} %copy-done.5, bf16[16,16,1,7,1,128]{5,3,4,1,0,2:T(8,128)(2,1)S(1)} %slice.16, bf16[16,16,1,8,3,128]{5,3,4,1,0,2:T(8,128)(2,1)S(1)} %copy.144), kind=kOutput, calls=%fused_computation.24 | convolution fusion | flops 332021760 | bytes 2873344 | tf_op jit(solution)/shard_map/conv_general_dilated | solution.py:42
  402.2 13.6 %copy.145 = bf16[32,32,8,6,8]{1,4,3,2,0:T(8,128)(2,1)S(1)} copy(bf16[32,32,8,6,8]{4,2,3,1,0:T(8,128)(2,1)} %fusion.17) | data formatting | bytes 1572864 | tf_op jit(solution)/shard_map/conv_general_dilated | solution.py:42
  419.7 4.9 all-to-all-start.1
  424.6 13.5 %copy.154 = bf16[1,16,16,16,128]{4,0,3,2,1:T(2,128)(2,1)S(1)} copy(bf16[1,16,16,16,128]{3,2,1,0,4:T(8,128)(2,1)} %all-gather.2.cloned.1.call-done) | data formatting | bytes 2097152 | tf_op jit(solution)/shard_map/all_gather | solution.py:77
  438.1 51.8 %fusion.36 = f32[3,3,3,8,128]{4,3,2,1,0:T(8,128)} fusion(bf16[1,32,32,32,8]{4,0,3,2,1:T(2,128)(2,1)} %copy.153, bf16[1,16,16,16,128]{4,0,3,2,1:T(2,128)(2,1)S(1)} %copy.154), kind=kOutput, calls=%fused_computation.46 | convolution fusion | flops 212629504 | bytes 1683456 | tf_op jit(solution)/shard_map/transpose | solution.py:37
  491.3 3.4 copy.147
  494.7 3.5 fusion.12
  498.2 4.1 copy.151
  502.3 46.6 %fusion.35 = f32[3,3,3,32,64]{4,3,2,1,0:T(8,128)} fusion(bf16[1,9,64,64,32]{4,0,3,2,1:T(2,128)(2,1)} %pad_maximum_fusion, bf16[1,4,32,32,64]{4,0,3,2,1:T(2,128)(2,1)} %copy.151), kind=kOutput, calls=%fused_computation.45 | convolution fusion | flops 443596800 | bytes 3104768 | tf_op jit(solution)/shard_map/transpose | solution.py:37
  550.5 14.3 %copy.156 = f32[1,16,16,16,128]{2,3,1,0,4:T(8,128)} copy(f32[1,16,16,16,128]{4,2,3,1,0:T(8,128)} %slice_bitcast_fusion.1) | data formatting | bytes 4194304
  564.8 15.3 %reshape.69 = f32[128,4096]{1,0:T(8,128)} reshape(f32[128,1,16,16,16]{4,3,2,1,0:T(8,128)} %bitcast.66) | data formatting | bytes 4194304
  580.1 45.1 %all-reduce.5.cloned.1.call-done = f32[3,3,3,8,128]{4,3,2,1,0:T(8,128)} async-done(((f32[3,3,3,8,128]{4,3,2,1,0:T(8,128)}), f32[3,3,3,8,128]{4,3,2,1,0:T(8,128)}) %all-reduce.5.cloned.1.call-update) | async-done | bytes 110608 | tf_op jit(solution)/shard_map/psum | solution.py:84
  626.8 147.3 %all-reduce.3.cloned.1.call-done = f32[3,3,3,32,64]{4,3,2,1,0:T(8,128)} async-done(((f32[3,3,3,32,64]{4,3,2,1,0:T(8,128)}), f32[3,3,3,32,64]{4,3,2,1,0:T(8,128)}) %all-reduce.3.cloned.1.call-update) | async-done | bytes 221200 | tf_op jit(solution)/shard_map/psum | solution.py:83
  775.9 51.3 %reduce-scatter.4.cloned.1.call-done = f32[16,4096]{1,0:T(8,128)} async-done(((f32[128,4096]{1,0:T(8,128)}), f32[16,4096]{1,0:T(8,128)}) %reduce-scatter.4.cloned.1.call-update) | async-done | bytes 262160
  (57 shorter events, 46.0 us)
Async XLA Ops:
  7.2 170.2 %copy-start = (bf16[3,3,3,32,64]{4,3,2,1,0:T(8,128)(2,1)S(1)}, bf16[3,3,3,32,64]{4,3,2,1,0:T(8,128)(2,1)}, u32[]{:S(2)}) copy-start(bf16[3,3,3,32,64]{4,3,2,1,0:T(8,128)(2,1)} %param.5) | copy-start | bytes 331780
  14.2 35.5 %collective-permute-start = (bf16[1,1,64,64,32]{3,4,2,1,0:T(8,128)(2,1)S(1)}, bf16[1,1,64,64,32]{3,4,2,1,0:T(8,128)(2,1)S(1)}, u32[]{:S(2)}, u32[]{:S(2)}) collective-permute-start(bf16[1,1,64,64,32]{3,4,2,1,0:T(8,128)(2,1)S(1)} %copy.125), channel_id=1, source_target_pairs={{0,16},{16,32},{32,48},{48,64},{64,80},{80,96},{96,112},{1,17},{17... | collective-permute-start | bytes 786440 | tf_op jit(solution)/shard_map/ppermute | solution.py:13
  175.0 2.4 copy-start.6
  195.8 10.1 %copy-start.3 = (f32[4,32,8,5,64]{4,2,3,1,0:T(8,128)S(1)}, f32[4,32,8,5,64]{4,2,3,1,0:T(8,128)}, u32[]{:S(2)}) copy-start(f32[4,32,8,5,64]{4,2,3,1,0:T(8,128)} %get-tuple-element.18) | copy-start | bytes 3932164
  195.8 15.0 %all-to-all-start = ((bf16[8,2,16384]{2,1,0:T(2,128)(2,1)}), bf16[8,2,16384]{2,1,0:T(2,128)(2,1)S(1)}, u32[]{:S(2)}, u32[]{:S(2)}) async-start(bf16[8,2,16384]{2,1,0:T(2,128)(2,1)} %reshape.71), calls=%async_computation | async-start | bytes 1048576 | tf_op jit(solution)/shard_map/all_to_all | solution.py:71
  202.0 174.8 %all-gather.2.cloned.1.call-start = ((), (), s32[]{:S(2)}) async-start(), calls=%async_computation.3 | async-start | bytes 9437184 | tf_op jit(solution)/shard_map/all_gather | solution.py:77
  237.2 3.4 copy-start.5
  237.2 3.5 copy-start.7
  402.2 13.6 %copy-start.4 = (pred[8,6]{1,0:T(8,128)(4,1)S(1)}, pred[8,6]{1,0:T(8,128)(4,1)}, u32[]{:S(2)}) copy-start(pred[8,6]{1,0:T(8,128)(4,1)} %constant.31) | copy-start | bytes 148
  419.7 70.3 %all-to-all-start.1 = ((bf16[8,2,16384]{2,1,0:T(2,128)(2,1)}), bf16[8,2,16384]{2,1,0:T(2,128)(2,1)S(1)}, u32[]{:S(2)}, u32[]{:S(2)}) async-start(bf16[8,2,16384]{2,1,0:T(2,128)(2,1)} %reshape.73), calls=%async_computation.1 | async-start | bytes 1048576 | tf_op jit(solution)/shard_map/all_to_all | solution.py:80
  424.6 200.6 %all-reduce.5.cloned.1.call-start = ((), (), s32[]{:S(2)}) async-start(), calls=%async_computation.5 | async-start | bytes 221184 | tf_op jit(solution)/shard_map/psum | solution.py:84
  489.9 284.1 %all-reduce.3.cloned.1.call-start = ((), (), s32[]{:S(2)}) async-start(), calls=%async_computation.4 | async-start | bytes 884736 | tf_op jit(solution)/shard_map/psum | solution.py:83
  502.3 46.7 %copy-start.2 = (f32[16,16,8,3,128]{4,1,3,2,0:T(8,128)S(1)}, f32[16,16,8,3,128]{4,1,3,2,0:T(8,128)}, u32[]{:S(2)}) copy-start(f32[16,16,8,3,128]{4,1,3,2,0:T(8,128)} %copy.139) | copy-start | bytes 9437188
  548.9 278.3 %reduce-scatter.4.cloned.1.call-start = ((), (), s32[]{:S(2)}) async-start(), calls=%async_computation.6 | async-start | bytes 2359296
  625.2 206.2 %copy-start.1 = (bf16[3,3,3,32,64]{4,3,2,1,0:T(8,128)(2,1)S(1)}, bf16[3,3,3,32,64]{4,3,2,1,0:T(8,128)(2,1)}, u32[]{:S(2)}) copy-start(bf16[3,3,3,32,64]{4,3,2,1,0:T(8,128)(2,1)} %param.5) | copy-start | bytes 331780
Sparse Core Ops, SparseCore 0:
  206.0 170.6 all-gather.1
  490.1 135.0 all-reduce.4
  631.2 142.7 all-reduce.2
  776.3 50.8 reduce-scatter.3
where the time goes:
time: 853 us; the launch traced here: 838 us
  waiting for transfers between devices  343 us (40%)
  local copies, waits for them, and re-layouts  263 us (31%)
  matrix products  137 us (16%)
  other arithmetic  66 us (8%)
  starting transfers between devices  15.2 us (2%)
  between operations  14.4 us (2%)
    psum x1, waiting for transfers between devices, shards(): total_a = lax.psum(local_a, ('mp', 'dp'))  147 us
    transpose x2, matrix products, kernel_grad(): return jnp.transpose(result, (1, 2, 3, 0, 4))  98.3 us
    all_gather x1, waiting for transfers between devices, shards(): upstream = lax.all_gather(cotangent, 'mp', axis=4, tiled=True)  97.7 us
    unnamed x32, local copies, waits for them, and re-layouts  66.3 us
    concatenate x1, other arithmetic, shards(): padded_x = pad_sides(jnp.concatenate([below, field], axis=1))  58.2 us
    unnamed x5, waiting for transfers between devices  51.4 us
    psum x1, waiting for transfers between devices, shards(): total_b = lax.psum(local_b, 'dp')  45.1 us
    concatenate x2, local copies, waits for them, and re-layouts, shards(): padded_x = pad_sides(jnp.concatenate([below, field], axis=1))  39.5 us
  transfers between devices with their start and end apart: 7, of which 5 were waited for; matrix products, arithmetic and copies ran while one was open for 32% of the time, Pallas kernels for 0%

commit v1 on v0

--- a/solution.py
+++ b/solution.py
@@ -80,7 +80,9 @@
     back = lax.all_to_all(back_group, "mp", split_axis=1, concat_axis=4, tiled=True)
     delta = (back.astype(jnp.float32) * jnp.where(pre > 0, 1.0, 0.3)).astype(jnp.bfloat16)
     local_a = kernel_grad(padded_x, delta)
-    total_a = lax.psum(local_a, ("mp", "dp"))
+    total_a = local_a
+    for over in ("dp", "mp"):
+        total_a = lax.psum(total_a, over)
     total_b = lax.psum(local_b, "dp")
     samples_all = samp_local * lax.axis_size("dp")
     grad_a = total_a / math.sqrt(samples_all * (GRID // 2) ** 3)

time: 853 us -> 736 us (0.86)
  waiting for transfers between devices: 343 us -> 228 us
    all_gather x1, waiting for transfers between devices: 97.7 us -> 0.01 us  [shards(): upstream = lax.all_gather(cotangent, 'mp', axis=4, tiled=True)]
    psum x2, waiting for transfers between devices: 192 us -> 167 us  [shards(): total_a = lax.psum(total_a, over)]
    unnamed x32 -> x34, local copies, waits for them, and re-layouts: 66.3 us -> 64.8 us
  transfers between devices with their start and end apart: 7 -> 7, of which waited for: 5 -> 4; matrix products, arithmetic and copies ran while one was open for 32% -> 49% of each run, Pallas kernels for 0% -> 0%
where the time goes in v1:
time: 736 us; the launch traced here: 722 us
  local copies, waits for them, and re-layouts  264 us (36%)
  waiting for transfers between devices  228 us (31%)
  matrix products  137 us (19%)
  other arithmetic  65.1 us (9%)
  between operations  14.3 us (2%)
  starting transfers between devices  13.5 us (2%)
    psum x2, waiting for transfers between devices, shards(): total_a = lax.psum(total_a, over)  167 us
    transpose x2, matrix products, kernel_grad(): return jnp.transpose(result, (1, 2, 3, 0, 4))  98.2 us
    unnamed x34, local copies, waits for them, and re-layouts  64.8 us
    concatenate x1, other arithmetic, shards(): padded_x = pad_sides(jnp.concatenate([below, field], axis=1))  58.2 us
    unnamed x5, waiting for transfers between devices  56.7 us
    concatenate x2, local copies, waits for them, and re-layouts, shards(): padded_x = pad_sides(jnp.concatenate([below, field], axis=1))  39.6 us
    conv_general_dilated x6, local copies, waits for them, and re-layouts, forward_conv(): lax.conv_general_dilated(padded, kernel, (2, 2, 2), 'VALID', dimension_nu...  38.5 us
    all_to_all x4, local copies, waits for them, and re-layouts, shards(): lax.all_to_all(hidden, 'mp', split_axis=4, concat_axis=1, tiled=True)  33.1 us
  transfers between devices with their start and end apart: 7, of which 4 were waited for; matrix products, arithmetic and copies ran while one was open for 49% of the time, Pallas kernels for 0%

profile of v1, /device:TPU:1, one launch (start us, length us, event | category | flops | bytes accessed | tf_op | source)
XLA Modules:
  0.0 722.3 jit_solution(4513401066225755487)
XLA Ops:
  7.2 4.9 copy.124
  14.3 4.0 collective-permute-start
  20.9 31.5 %copy.127 = bf16[1,8,64,64,32]{4,0,3,2,1:T(2,128)(2,1)} copy(bf16[1,8,64,64,32]{2,4,3,1,0:T(8,128)(2,1)} %bitcast.69) | data formatting | bytes 4194304 | tf_op jit(solution)/shard_map/reshape | solution.py:66
  55.0 58.2 %pad_maximum_fusion = bf16[1,9,64,64,32]{4,0,3,2,1:T(2,128)(2,1)} fusion(bf16[1,8,64,64,32]{4,0,3,2,1:T(2,128)(2,1)} %copy.127, bf16[1,1,64,64,32]{4,0,3,2,1:T(2,128)(2,1)S(1)} %copy.126), kind=kLoop, calls=%fused_computation.4 | loop fusion | flops 1179648 | bytes 4718592 | tf_op jit(solution)/shard_map/concatenate | solution.py:68
  113.2 33.6 %copy.128 = bf16[1,9,64,64,32]{3,4,2,1,0:T(8,128)(2,1)} copy(bf16[1,9,64,64,32]{4,0,3,2,1:T(2,128)(2,1)} %pad_maximum_fusion) | data formatting | bytes 4718592 | tf_op jit(solution)/shard_map/concatenate | solution.py:68
  146.8 9.2 %copy.159 = bf16[9,64,1,64,32]{1,4,3,0,2:T(8,128)(2,1)} copy(bf16[9,64,1,64,32]{3,4,2,1,0:T(8,128)(2,1)} %bitcast.72) | data formatting | bytes 4718592
  156.0 6.1 pad.4.clone
  162.1 15.6 %copy.131 = bf16[9,64,1,8,10,32]{5,3,4,1,0,2:T(8,128)(2,1)} copy(bf16[9,64,1,8,10,32]{1,5,4,3,0,2:T(8,128)(2,1)} %bitcast.67) | data formatting | bytes 5898240 | tf_op jit(solution)/shard_map/conv_general_dilated | solution.py:17
  180.1 12.0 %compare_select_fusion = (f32[4,32,8,5,64]{4,2,3,1,0:T(8,128)}, bf16[4,32,8,5,64]{4,2,3,1,0:T(8,128)(2,1)S(1)}) fusion(pred[8,5]{0,1:T(8,128)(4,1)S(1)} %copy-done.7, bf16[3,3,3,32,64]{4,3,2,1,0:T(8,128)(2,1)S(1)} %copy-done, bf16[9,64,1,7,2,32]{5,3,4,1,0,2:T(8,128)(2,1)S(1)} %slice.12, bf16[9,64,1,8,10,32]{5,3,4,1,0,2:T(8,128)(2,1)} %copy.131), kind=kOutput, calls=%fused_computation.20 | convolution fusion | flops 572915712 | bytes 5541928 | tf_op jit(solution)/shard_map/conv_general_dilated | solution.py:17
  198.7 5.9 all-to-all-start
  209.8 3.6 all-to-all-done
  219.5 3.4 copy.160
  223.0 4.0 pad.6.clone
  227.0 12.8 %copy.138 = bf16[32,32,1,8,6,8]{5,3,4,1,0,2:T(8,128)(2,1)} copy(bf16[32,32,1,8,6,8]{1,5,4,3,0,2:T(8,128)(2,1)} %bitcast.73) | data formatting | bytes 1572864 | tf_op jit(solution)/shard_map/conv_general_dilated | solution.py:17
  239.8 5.6 slice.14
  245.4 24.0 %copy.153 = bf16[1,32,32,32,8]{4,0,3,2,1:T(2,128)(2,1)} copy(bf16[1,32,32,32,8]{3,4,2,1,0:T(8,128)(2,1)S(1)} %bitcast.71) | data formatting | bytes 1048576 | tf_op jit(solution)/shard_map/all_to_all | solution.py:71
  269.4 10.0 %copy.141 = bf16[1,16,16,16,128]{4,3,2,1,0:T(8,128)(2,1)S(1)} copy(bf16[1,16,16,16,128]{3,2,1,0,4:T(8,128)(2,1)} %all-gather.2.cloned.1.call-done) | data formatting | bytes 2097152 | tf_op jit(solution)/shard_map/all_gather | solution.py:77
  280.6 14.0 %fusion.17 = bf16[32,32,8,6,8]{4,2,3,1,0:T(8,128)(2,1)} fusion(bf16[3,3,3,8,128]{4,3,2,1,0:T(8,128)(2,1)S(1)} %copy-done.5, bf16[16,16,1,7,1,128]{5,3,4,1,0,2:T(8,128)(2,1)S(1)} %slice.16, bf16[16,16,1,8,3,128]{5,3,4,1,0,2:T(8,128)(2,1)S(1)} %copy.144), kind=kOutput, calls=%fused_computation.24 | convolution fusion | flops 332021760 | bytes 2873344 | tf_op jit(solution)/shard_map/conv_general_dilated | solution.py:42
  294.6 13.6 %copy.145 = bf16[32,32,8,6,8]{1,4,3,2,0:T(8,128)(2,1)S(1)} copy(bf16[32,32,8,6,8]{4,2,3,1,0:T(8,128)(2,1)} %fusion.17) | data formatting | bytes 1572864 | tf_op jit(solution)/shard_map/conv_general_dilated | solution.py:42
  312.1 3.5 all-to-all-start.1
  315.7 13.9 %copy.154 = bf16[1,16,16,16,128]{4,0,3,2,1:T(2,128)(2,1)S(1)} copy(bf16[1,16,16,16,128]{3,2,1,0,4:T(8,128)(2,1)} %all-gather.2.cloned.1.call-done) | data formatting | bytes 2097152 | tf_op jit(solution)/shard_map/all_gather | solution.py:77
  329.6 51.8 %fusion.36 = f32[3,3,3,8,128]{4,3,2,1,0:T(8,128)} fusion(bf16[1,32,32,32,8]{4,0,3,2,1:T(2,128)(2,1)} %copy.153, bf16[1,16,16,16,128]{4,0,3,2,1:T(2,128)(2,1)S(1)} %copy.154), kind=kOutput, calls=%fused_computation.46 | convolution fusion | flops 212629504 | bytes 1683456 | tf_op jit(solution)/shard_map/transpose | solution.py:37
  382.4 3.4 copy.147
  385.9 3.5 fusion.12
  389.4 4.0 copy.151
  393.4 46.5 %fusion.35 = f32[3,3,3,32,64]{4,3,2,1,0:T(8,128)} fusion(bf16[1,9,64,64,32]{4,0,3,2,1:T(2,128)(2,1)} %pad_maximum_fusion, bf16[1,4,32,32,64]{4,0,3,2,1:T(2,128)(2,1)} %copy.151), kind=kOutput, calls=%fused_computation.45 | convolution fusion | flops 443596800 | bytes 3104768 | tf_op jit(solution)/shard_map/transpose | solution.py:37
  440.0 13.0 %broadcast_select_fusion = f32[16,16,8,3,128]{4,2,3,1,0:T(8,128)S(1)} fusion(pred[8,3]{0,1:T(4,128)(4,1)S(1)} %copy-done.8, bf16[3,3,3,8,128]{4,3,2,1,0:T(8,128)(2,1)S(1)} %copy-done.6, bf16[32,32,1,7,2,8]{5,3,4,1,0,2:T(8,128)(2,1)} %slice.14, bf16[32,32,1,8,6,8]{5,3,4,1,0,2:T(8,128)(2,1)} %copy.138), kind=kOutput, calls=%fused_computation.30 | convolution fusion | flops 329662464 | bytes 4216856 | tf_op jit(solution)/shard_map/conv_general_dilated | solution.py:17
  453.6 125.6 %all-reduce.6.cloned.1.call-done = (f32[3,3,3,32,64]{4,3,2,1,0:T(8,128)}, f32[3,3,3,8,128]{4,3,2,1,0:T(8,128)}) async-done(((f32[3,3,3,32,64]{4,3,2,1,0:T(8,128)}, f32[3,3,3,8,128]{4,3,2,1,0:T(8,128)}), (f32[3,3,3,32,64]{4,3,2,1,0:T(8,128)}, f32[3,3,3,8,128]{4,3,2,1,0:T(8,128)})) %all-reduce.6.cloned.1.call-update) | async-done | bytes 331792 | tf_op jit(solution)/shard_map/psum | solution.py:85
  580.8 14.3 %copy.156 = f32[1,16,16,16,128]{2,3,1,0,4:T(8,128)} copy(f32[1,16,16,16,128]{4,2,3,1,0:T(8,128)} %slice_bitcast_fusion.1) | data formatting | bytes 4194304
  595.0 15.3 %reshape.69 = f32[128,4096]{1,0:T(8,128)} reshape(f32[128,1,16,16,16]{4,3,2,1,0:T(8,128)} %bitcast.66) | data formatting | bytes 4194304
  611.1 41.9 %all-reduce.4.cloned.1.call-done = f32[3,3,3,32,64]{4,3,2,1,0:T(8,128)} async-done(((f32[3,3,3,32,64]{4,3,2,1,0:T(8,128)}), f32[3,3,3,32,64]{4,3,2,1,0:T(8,128)}) %all-reduce.4.cloned.1.call-update) | async-done | bytes 221200 | tf_op jit(solution)/shard_map/psum | solution.py:85
  654.8 56.6 %reduce-scatter.4.cloned.1.call-done = f32[16,4096]{1,0:T(8,128)} async-done(((f32[128,4096]{1,0:T(8,128)}), f32[16,4096]{1,0:T(8,128)}) %reduce-scatter.4.cloned.1.call-update) | async-done | bytes 262160
  (59 shorter events, 42.7 us)
Async XLA Ops:
  7.2 172.9 %copy-start = (bf16[3,3,3,32,64]{4,3,2,1,0:T(8,128)(2,1)S(1)}, bf16[3,3,3,32,64]{4,3,2,1,0:T(8,128)(2,1)}, u32[]{:S(2)}) copy-start(bf16[3,3,3,32,64]{4,3,2,1,0:T(8,128)(2,1)} %param.5) | copy-start | bytes 331780
  7.2 11.1 %copy-start.2 = (bf16[1,16,16,16,16]{4,3,2,1,0:T(8,128)(2,1)S(1)}, bf16[1,16,16,16,16]{4,3,2,1,0:T(8,128)(2,1)}, u32[]{:S(2)}) copy-start(bf16[1,16,16,16,16]{4,3,2,1,0:T(8,128)(2,1)} %param.7) | copy-start | bytes 393220
  7.2 262.2 %all-gather.2.cloned.1.call-start = ((), (), s32[]{:S(2)}) async-start(), calls=%async_computation.3 | async-start | bytes 9437184 | tf_op jit(solution)/shard_map/all_gather | solution.py:77
  14.3 38.1 %collective-permute-start = (bf16[1,1,64,64,32]{3,4,2,1,0:T(8,128)(2,1)S(1)}, bf16[1,1,64,64,32]{3,4,2,1,0:T(8,128)(2,1)S(1)}, u32[]{:S(2)}, u32[]{:S(2)}) collective-permute-start(bf16[1,1,64,64,32]{3,4,2,1,0:T(8,128)(2,1)S(1)} %copy.125), channel_id=1, source_target_pairs={{0,16},{16,32},{32,48},{48,64},{64,80},{80,96},{96,112},{1,17},{17... | collective-permute-start | bytes 786440 | tf_op jit(solution)/shard_map/ppermute | solution.py:13
  177.8 2.4 copy-start.7
  198.7 14.8 %all-to-all-start = ((bf16[8,2,16384]{2,1,0:T(2,128)(2,1)}), bf16[8,2,16384]{2,1,0:T(2,128)(2,1)S(1)}, u32[]{:S(2)}, u32[]{:S(2)}) async-start(bf16[8,2,16384]{2,1,0:T(2,128)(2,1)} %reshape.71), calls=%async_computation | async-start | bytes 1048576 | tf_op jit(solution)/shard_map/all_to_all | solution.py:71
  279.7 0.9 copy-start.5
  294.6 13.6 %copy-start.4 = (pred[8,6]{1,0:T(8,128)(4,1)S(1)}, pred[8,6]{1,0:T(8,128)(4,1)}, u32[]{:S(2)}) copy-start(pred[8,6]{1,0:T(8,128)(4,1)} %constant.31) | copy-start | bytes 148
  312.1 69.3 %all-to-all-start.1 = ((bf16[8,2,16384]{2,1,0:T(2,128)(2,1)}), bf16[8,2,16384]{2,1,0:T(2,128)(2,1)S(1)}, u32[]{:S(2)}, u32[]{:S(2)}) async-start(bf16[8,2,16384]{2,1,0:T(2,128)(2,1)} %reshape.73), calls=%async_computation.1 | async-start | bytes 1048576 | tf_op jit(solution)/shard_map/all_to_all | solution.py:80
  315.6 263.5 %all-reduce.6.cloned.1.call-start = ((), (), s32[]{:S(2)}) async-start(), calls=%async_computation.6 | async-start | bytes 1105920 | tf_op jit(solution)/shard_map/psum | solution.py:85
  393.4 46.5 %copy-start.6 = (bf16[3,3,3,8,128]{4,3,2,1,0:T(8,128)(2,1)S(1)}, bf16[3,3,3,8,128]{4,3,2,1,0:T(8,128)(2,1)}, u32[]{:S(2)}) copy-start(bf16[3,3,3,8,128]{4,3,2,1,0:T(8,128)(2,1)} %param.6) | copy-start | bytes 165892
  393.4 46.6 %copy-start.8 = (pred[8,3]{0,1:T(4,128)(4,1)S(1)}, pred[8,3]{0,1:T(4,128)(4,1)}, u32[]{:S(2)}) copy-start(pred[8,3]{0,1:T(4,128)(4,1)} %constant.29) | copy-start | bytes 76
  439.9 213.0 %all-reduce.4.cloned.1.call-start = ((), (), s32[]{:S(2)}) async-start(), calls=%async_computation.4 | async-start | bytes 884736 | tf_op jit(solution)/shard_map/psum | solution.py:85
  579.2 132.2 %reduce-scatter.4.cloned.1.call-start = ((), (), s32[]{:S(2)}) async-start(), calls=%async_computation.5 | async-start | bytes 2359296
  595.0 15.3 %copy-start.3 = (f32[3,3,3,8,128]{4,3,2,1,0:T(8,128)S(1)}, f32[3,3,3,8,128]{4,3,2,1,0:T(8,128)}, u32[]{:S(2)}) copy-start(f32[3,3,3,8,128]{4,3,2,1,0:T(8,128)} %get-tuple-element.19) | copy-start | bytes 331780
  610.4 105.2 %copy-start.1 = (bf16[3,3,3,32,64]{4,3,2,1,0:T(8,128)(2,1)S(1)}, bf16[3,3,3,32,64]{4,3,2,1,0:T(8,128)(2,1)}, u32[]{:S(2)}) copy-start(bf16[3,3,3,32,64]{4,3,2,1,0:T(8,128)(2,1)} %param.5) | copy-start | bytes 331780
Sparse Core Ops, SparseCore 0:
  21.0 170.8 all-gather.1
  440.0 139.0 all-reduce.5
  581.8 71.0 all-reduce.3
  655.2 56.1 reduce-scatter.3
